TPU v7x, 32 devices: a whole 2x2x4 slice. The times are simulated.
32 devices in a mesh: expert: 8 (over z, y), wshard: 4 (over x, core).
Axes of the slice: x: 2, y: 2, z: 4, core: 2. Of those that a mesh axis runs over, the one named last changes fastest.
Arguments:
- tokens: bfloat16 [16384, 768], P(('expert', 'wshard')), may hold values from -6 to 6
- attn_norm: bfloat16 [768], P('wshard'), may hold values from 0.5 to 1.5
- attn_in: bfloat16 [768, 2304], P('wshard'), may hold values from -0.21875 to 0.21875
- attn_out: bfloat16 [768, 768], P('wshard'), may hold values from -6 to 6
- rel_bias: bfloat16 [32, 12], replicated, may hold values from -6 to 6
- buckets: int32 [4095], replicated, may hold values from 0 to 31
- ffn_norm: bfloat16 [768], P('wshard'), may hold values from 0.5 to 1.5
- router: bfloat16 [768, 8], P('wshard'), may hold values from -0.375 to 0.375
- routes: int32 [16384, 1], P(('expert', 'wshard')), may hold values from 0 to 7; in each aligned block of 512 rows (0 to 511, 512 to 1023, ...) at most 128 rows name the same one
- expert_in: bfloat16 [8, 768, 3072], P('expert'), may hold values from -0.21875 to 0.21875
- expert_out: bfloat16 [8, 3072, 768], P('expert'), may hold values from -2 to 2
- cotangent: bfloat16 [16384, 768], P(('expert', 'wshard')), may hold values from -6 to 6
Outputs:
- mixed: bfloat16 [16384, 768], P(('expert', 'wshard'))
- grad_tokens: float32 [16384, 768], P(('expert', 'wshard'))
- grad_attn_norm: float32 [768], P(('expert', 'wshard'))
- grad_attn_in: float32 [768, 2304], P(('expert', 'wshard'))
- grad_attn_out: float32 [768, 768], P(('expert', 'wshard'))
- grad_rel_bias: float32 [32, 12], replicated
- grad_ffn_norm: float32 [768], P(('expert', 'wshard'))
- grad_router: float32 [768, 8], P(('expert', 'wshard'))
- grad_expert_in: float32 [8, 768, 3072], P('expert', None, 'wshard')
- grad_expert_out: float32 [8, 3072, 768], P('expert', 'wshard')
Inputs may be any that keep to these rules, and one draw needn't show every extreme that they name: `routes`: among the rows of one device no expert is named by more than 128 rows, and on some device some expert is named by exactly 128.
All inputs are finite; a program needn't handle non-finite values.
Results may differ from a plain program's by a relative error of at most 0.015.
Values may be sent and summed in bfloat16 or wider, within the bound.
No kernel may reach another device: no remote copies, remote signals or barrier semaphores. Data moves between devices by JAX's collectives and lax.ppermute only.
A program may use at most 256 MiB of HBM per device.

v0:
```python
import jax
import jax.numpy as jnp
from jax import lax
from jax.sharding import PartitionSpec as P

epsilon = 1e-06
highest = lax.Precision.HIGHEST


def rms_scale(values):
    return lax.rsqrt(jnp.mean(values * values, axis=-1, keepdims=True) + epsilon)


def norm_back(grad_normed, values, scale, gain):
    scaled = grad_normed * gain
    inner_mean = jnp.mean(scaled * values, axis=-1, keepdims=True)
    grad_values = scale * scaled - values * (scale * scale * scale) * inner_mean
    return (grad_values, jnp.sum(grad_normed * values * scale, axis=0))


def expand_offsets(offset_rows, row_count, col_count):
    head_count = offset_rows.shape[0]
    span = row_count + col_count
    padded = jnp.pad(offset_rows, ((0, 0), (0, 1)))
    repeated = jnp.tile(padded, (1, row_count))[:, : row_count * (span - 1)]
    return repeated.reshape(head_count, row_count, span - 1)[:, :, row_count - 1 :]


def fold_offsets(score_grid):
    head_count, row_count, col_count = score_grid.shape
    span = row_count + col_count
    placed = jnp.pad(score_grid, ((0, 0), (0, 0), (row_count - 1, 0)))
    flattened = jnp.pad(
        placed.reshape(head_count, row_count * (span - 1)), ((0, 0), (0, row_count))
    )
    return jnp.sum(flattened.reshape(head_count, row_count, span), axis=1)[:, : span - 1]


def head_groups(rows, head_count, group_size):
    row_count, width = rows.shape
    head_size = width // head_count
    return rows.reshape(row_count, head_count // group_size, group_size, head_size).transpose(
        1, 0, 2, 3
    )


def ungroup(grouped):
    group_total, row_count, group_size, head_size = grouped.shape
    return grouped.transpose(1, 0, 2, 3).reshape(row_count, group_total * group_size * head_size)


def block_scores(query_heads, key_heads, offset_bias, global_start):
    length = key_heads.shape[0]
    row_count = query_heads.shape[0]
    raw_scores = (
        jnp.einsum("qhd,khd->hqk", query_heads, key_heads, preferred_element_type=jnp.float32)
        * 0.125
    )
    bias_rows = lax.dynamic_slice_in_dim(
        offset_bias, length - row_count - global_start, row_count + length - 1, 1
    )
    return raw_scores + expand_offsets(bias_rows, row_count, length)


def attention_forward(query_groups, key_groups, value_groups, bias_groups, block_rows, row_base):

    def per_group(items):
        query_group, key_group, value_group, bias_group = items
        local_rows = query_group.shape[0]

        def one_block(block_index):
            row_start = block_index * block_rows
            scores = block_scores(query_group, key_group, bias_group, row_base + row_start)
            row_max = jnp.max(scores, axis=-1, keepdims=True)
            exp_scores = jnp.exp(scores - row_max)
            row_total = jnp.sum(exp_scores, axis=-1, keepdims=True)
            probs_low = (exp_scores / row_total).astype(jnp.bfloat16)
            mixed_part = jnp.einsum(
                "hqk,khd->qhd", probs_low, value_group, preferred_element_type=jnp.float32
            )
            return (mixed_part.astype(jnp.bfloat16), (row_max + jnp.log(row_total))[:, :, 0])

        mixed_parts, log_totals = lax.map(one_block, jnp.arange(local_rows // block_rows))
        return (
            mixed_parts.reshape(local_rows, mixed_parts.shape[2], mixed_parts.shape[3]),
            log_totals,
        )

    return lax.map(per_group, (query_groups, key_groups, value_groups, bias_groups))


def attention_backward(
    query_groups,
    key_groups,
    value_groups,
    bias_groups,
    log_groups,
    grad_groups,
    block_rows,
    row_base,
):

    def per_group(items):
        query_group, key_group, value_group, bias_group, log_group, grad_group = items
        local_rows = query_group.shape[0]
        length = key_group.shape[0]
        span = block_rows + length - 1

        def one_block(totals, inputs):
            block_index, block_logs = inputs
            grad_keys, grad_values, grad_offsets = totals
            row_start = block_index * block_rows
            global_start = row_base + row_start
            scores = block_scores(query_group, key_group, bias_group, global_start)
            weights = jnp.exp(scores - block_logs[:, :, None])
            grad_weights = jnp.einsum(
                "qhd,khd->hqk", grad_group, value_group, preferred_element_type=jnp.float32
            )
            grad_values = grad_values + jnp.einsum(
                "hqk,qhd->khd",
                weights.astype(jnp.bfloat16),
                grad_group,
                preferred_element_type=jnp.float32,
            )
            grad_scores = weights * (
                grad_weights - jnp.sum(grad_weights * weights, axis=-1, keepdims=True)
            )
            offset_start = length - block_rows - global_start
            current = lax.dynamic_slice_in_dim(grad_offsets, offset_start, span, 1)
            grad_offsets = lax.dynamic_update_slice_in_dim(
                grad_offsets, current + fold_offsets(grad_scores), offset_start, 1
            )
            scores_low = grad_scores.astype(jnp.bfloat16)
            grad_query = (
                jnp.einsum(
                    "hqk,khd->qhd", scores_low, key_group, preferred_element_type=jnp.float32
                )
                * 0.125
            )
            grad_keys = (
                grad_keys
                + jnp.einsum(
                    "hqk,qhd->khd", scores_low, query_group, preferred_element_type=jnp.float32
                )
                * 0.125
            )
            return ((grad_keys, grad_values, grad_offsets), grad_query)

        zero_heads = jnp.zeros(key_group.shape, jnp.float32)
        start_totals = (zero_heads, zero_heads, jnp.zeros(bias_group.shape, jnp.float32))
        final_totals, grad_queries = lax.scan(
            one_block, start_totals, (jnp.arange(local_rows // block_rows), log_group)
        )
        grad_keys, grad_values, grad_offsets = final_totals
        return (
            grad_queries.reshape(local_rows, grad_queries.shape[2], grad_queries.shape[3]),
            grad_keys,
            grad_values,
            grad_offsets,
        )

    return lax.map(
        per_group, (query_groups, key_groups, value_groups, bias_groups, log_groups, grad_groups)
    )


def expert_forward(expert_rows, weight_in, weight_out):
    inner_act = jnp.einsum(
        "secd,edf->secf", expert_rows, weight_in, preferred_element_type=jnp.float32
    )
    hidden_act = jax.nn.gelu(inner_act).astype(jnp.bfloat16)
    return (
        inner_act,
        hidden_act,
        jnp.einsum("secf,efd->secd", hidden_act, weight_out, preferred_element_type=jnp.float32),
    )


def expert_backward(expert_rows, inner_act, hidden_act, grad_rows, weight_in, weight_out):
    grad_hidden = jnp.einsum(
        "secd,efd->secf", grad_rows, weight_out, preferred_element_type=jnp.float32
    )
    unused, pullback = jax.vjp(jax.nn.gelu, inner_act)
    grad_inner = pullback(grad_hidden)[0].astype(jnp.bfloat16)
    grad_weight_out = jnp.einsum(
        "secf,secd->efd", hidden_act, grad_rows, preferred_element_type=jnp.float32
    )
    grad_weight_in = jnp.einsum(
        "secd,secf->edf", expert_rows, grad_inner, preferred_element_type=jnp.float32
    )
    grad_inputs = jnp.einsum(
        "secf,edf->secd", grad_inner, weight_in, preferred_element_type=jnp.float32
    )
    return (grad_weight_in, grad_weight_out, grad_inputs)


def to_slots(rows, slot_index, slot_count, capacity):
    empty_slots = jnp.zeros((slot_count * capacity, rows.shape[1]), rows.dtype)
    return empty_slots.at[slot_index].set(rows).reshape(slot_count, capacity, rows.shape[1])


def local(
    tokens,
    attn_norm,
    attn_in,
    attn_out,
    rel_bias,
    buckets,
    ffn_norm,
    router,
    routes,
    expert_in,
    expert_out,
    cotangent,
):
    full_norm_a, full_in, full_out, full_norm_f, full_router = (
        lax.all_gather(attn_norm, "wshard", axis=0, tiled=True),
        lax.all_gather(attn_in, "wshard", axis=0, tiled=True),
        lax.all_gather(attn_out, "wshard", axis=0, tiled=True),
        lax.all_gather(ffn_norm, "wshard", axis=0, tiled=True),
        lax.all_gather(router, "wshard", axis=0, tiled=True),
    )
    length, model_width = tokens.shape
    bucket_count, head_count = rel_bias.shape
    group_size = min(4, head_count)
    block_rows = min(512, length)
    row_base = lax.axis_index("wshard") * length
    start_rows = tokens.astype(jnp.float32)
    scale_a = rms_scale(start_rows)
    gain_a = full_norm_a.astype(jnp.float32)
    normed = (start_rows * scale_a * gain_a).astype(jnp.bfloat16)
    qkv = jnp.dot(normed, full_in, preferred_element_type=jnp.float32).astype(jnp.bfloat16)
    seq_keys, seq_values = (
        lax.all_gather(qkv[:, model_width : 2 * model_width], "wshard", axis=0, tiled=True),
        lax.all_gather(qkv[:, 2 * model_width :], "wshard", axis=0, tiled=True),
    )
    bucket_table = (buckets[:, None] == jnp.arange(bucket_count, dtype=jnp.int32)[None, :]).astype(
        jnp.float32
    )
    offset_bias = jnp.einsum(
        "ob,bh->ho", bucket_table, rel_bias.astype(jnp.float32), precision=highest
    )
    bias_groups = offset_bias.reshape(head_count // group_size, group_size, offset_bias.shape[1])
    query_groups = head_groups(qkv[:, :model_width], head_count, group_size)
    key_groups = head_groups(seq_keys, head_count, group_size)
    value_groups = head_groups(seq_values, head_count, group_size)
    mixed_groups, log_groups = attention_forward(
        query_groups, key_groups, value_groups, bias_groups, block_rows, row_base
    )
    mixed_heads = ungroup(mixed_groups)
    branch = jnp.dot(mixed_heads, full_out, preferred_element_type=jnp.float32)
    middle = start_rows + branch
    scale_f = rms_scale(middle)
    gain_f = full_norm_f.astype(jnp.float32)
    normed_f = (middle * scale_f * gain_f).astype(jnp.bfloat16)
    logits = jnp.dot(normed_f, full_router, preferred_element_type=jnp.float32)
    shifted = jnp.exp(logits - jnp.max(logits, axis=-1, keepdims=True))
    router_probs = shifted / jnp.sum(shifted, axis=-1, keepdims=True)
    experts_total = full_router.shape[1]
    route_ids = routes[:, 0]
    route_hot = route_ids[:, None] == jnp.arange(experts_total, dtype=jnp.int32)[None, :]
    hot_counts = route_hot.astype(jnp.int32)
    gate_prob = jnp.sum(jnp.where(route_hot, router_probs, 0.0), axis=-1, keepdims=True)
    capacity = max(2, 2 * length // experts_total)
    slot_rank = jnp.sum((jnp.cumsum(hot_counts, axis=0) - 1) * hot_counts, axis=1)
    slot_index = route_ids * capacity + slot_rank
    local_experts = expert_in.shape[0]
    sources = experts_total // local_experts
    outgoing = to_slots(normed_f, slot_index, experts_total, capacity)
    arrived = lax.all_to_all(outgoing, "expert", split_axis=0, concat_axis=0, tiled=True).reshape(
        sources, local_experts, capacity, model_width
    )
    inner_act, hidden_act, pieces_out = expert_forward(arrived, expert_in, expert_out)
    results = pieces_out.astype(jnp.bfloat16)
    returned = lax.all_to_all(
        results.reshape(experts_total, capacity, model_width),
        "expert",
        split_axis=0,
        concat_axis=0,
        tiled=True,
    )
    expert_result = returned.reshape(experts_total * capacity, model_width)[slot_index].astype(
        jnp.float32
    )
    mixed = (middle + gate_prob * expert_result).astype(jnp.bfloat16)
    grad_out = cotangent.astype(jnp.float32)
    grad_gate = jnp.sum(grad_out * expert_result, axis=-1, keepdims=True)
    grad_result = (gate_prob * grad_out).astype(jnp.bfloat16)
    grad_outgoing = to_slots(grad_result, slot_index, experts_total, capacity)
    grad_arrived = lax.all_to_all(
        grad_outgoing, "expert", split_axis=0, concat_axis=0, tiled=True
    ).reshape(sources, local_experts, capacity, model_width)
    local_in, local_out, grad_pieces = expert_backward(
        arrived, inner_act, hidden_act, grad_arrived, expert_in, expert_out
    )
    grad_expert_in, grad_expert_out = (
        lax.psum_scatter(
            local_in.astype(jnp.bfloat16), "wshard", scatter_dimension=2, tiled=True
        ).astype(jnp.float32),
        lax.psum_scatter(
            local_out.astype(jnp.bfloat16), "wshard", scatter_dimension=1, tiled=True
        ).astype(jnp.float32),
    )
    grad_expert_rows = grad_pieces.astype(jnp.bfloat16)
    grad_returned = lax.all_to_all(
        grad_expert_rows.reshape(experts_total, capacity, model_width),
        "expert",
        split_axis=0,
        concat_axis=0,
        tiled=True,
    )
    grad_expert_path = grad_returned.reshape(experts_total * capacity, model_width)[
        slot_index
    ].astype(jnp.float32)
    grad_logits = router_probs * (jnp.where(route_hot, grad_gate, 0.0) - gate_prob * grad_gate)
    logits_low = grad_logits.astype(jnp.bfloat16)
    grad_router = jnp.einsum("td,te->de", normed_f, logits_low, preferred_element_type=jnp.float32)
    grad_normed_f = (
        jnp.einsum("te,de->td", logits_low, full_router, preferred_element_type=jnp.float32)
        + grad_expert_path
    )
    grad_middle_norm, grad_gain_f = norm_back(grad_normed_f, middle, scale_f, gain_f)
    grad_middle = grad_out + grad_middle_norm
    grad_branch = grad_middle.astype(jnp.bfloat16)
    grad_attn_out = jnp.einsum(
        "td,te->de", mixed_heads, grad_branch, preferred_element_type=jnp.float32
    )
    grad_mixed = jnp.einsum(
        "te,de->td", grad_branch, full_out, preferred_element_type=jnp.float32
    ).astype(jnp.bfloat16)
    grad_mixed_groups = head_groups(grad_mixed, head_count, group_size)
    grad_query_groups, grad_key_groups, grad_value_groups, grad_offset_groups = attention_backward(
        query_groups,
        key_groups,
        value_groups,
        bias_groups,
        log_groups,
        grad_mixed_groups,
        block_rows,
        row_base,
    )
    local_keys, local_values = (
        lax.psum_scatter(
            ungroup(grad_key_groups).astype(jnp.bfloat16), "wshard", scatter_dimension=0, tiled=True
        ).astype(jnp.float32),
        lax.psum_scatter(
            ungroup(grad_value_groups).astype(jnp.bfloat16),
            "wshard",
            scatter_dimension=0,
            tiled=True,
        ).astype(jnp.float32),
    )
    qkv_low = jnp.concatenate(
        [ungroup(grad_query_groups), local_keys, local_values], axis=1
    ).astype(jnp.bfloat16)
    grad_offsets = grad_offset_groups.reshape(head_count, grad_offset_groups.shape[2])
    grad_attn_in = jnp.einsum("td,te->de", normed, qkv_low, preferred_element_type=jnp.float32)
    grad_normed = jnp.einsum("te,de->td", qkv_low, full_in, preferred_element_type=jnp.float32)
    grad_start, grad_gain_a = norm_back(grad_normed, start_rows, scale_a, gain_a)
    grad_tokens = grad_middle + grad_start
    local_bias = jnp.einsum("ob,ho->bh", bucket_table, grad_offsets, precision=highest)
    grad_rel_bias = lax.psum(local_bias, ("expert", "wshard"))
    sum_gain_a, sum_attn_in, sum_attn_out, sum_gain_f, sum_router = (
        lax.psum_scatter(grad_gain_a, ("expert", "wshard"), scatter_dimension=0, tiled=True),
        lax.psum_scatter(grad_attn_in, ("expert", "wshard"), scatter_dimension=0, tiled=True),
        lax.psum_scatter(grad_attn_out, ("expert", "wshard"), scatter_dimension=0, tiled=True),
        lax.psum_scatter(grad_gain_f, ("expert", "wshard"), scatter_dimension=0, tiled=True),
        lax.psum_scatter(grad_router, ("expert", "wshard"), scatter_dimension=0, tiled=True),
    )
    return (
        mixed,
        grad_tokens,
        sum_gain_a,
        sum_attn_in,
        sum_attn_out,
        grad_rel_bias,
        sum_gain_f,
        sum_router,
        grad_expert_in,
        grad_expert_out,
    )


def solution(mesh):
    placed = (
        P(("expert", "wshard"), None),
        P("wshard"),
        P("wshard", None),
        P("wshard", None),
        P(),
        P(),
        P("wshard"),
        P("wshard", None),
        P(("expert", "wshard"), None),
        P("expert", None, None),
        P("expert", None, None),
        P(("expert", "wshard"), None),
    )
    return jax.shard_map(
        local,
        mesh=mesh,
        in_specs=placed,
        out_specs=(
            P(("expert", "wshard"), None),
            P(("expert", "wshard"), None),
            P(("expert", "wshard")),
            P(("expert", "wshard"), None),
            P(("expert", "wshard"), None),
            P(),
            P(("expert", "wshard")),
            P(("expert", "wshard"), None),
            P("expert", None, "wshard"),
            P("expert", "wshard", None),
        ),
        check_vma=False,
    )
```

profile of v0, /device:TPU:0, one launch (start us, length us, event | category | flops | bytes accessed | tf_op | source)
XLA Modules:
  0.0 1997.7 jit_solution(12315147785937737854)
XLA Ops:
  21.9 21.2 %all-gather.6.cloned.1.call-done = bf16[768,2304]{1,0:T(8,128)(2,1)} async-done(((bf16[192,2304]{1,0:T(8,128)(2,1)}), bf16[768,2304]{1,0:T(8,128)(2,1)}) %all-gather.6.cloned.1.call-update) | async-done | bytes 3538960 | tf_op jit(solution)/shard_map/all_gather | solution.py:218
  54.9 22.6 %all-gather.10.cloned.1.call-done = bf16[2048,768]{1,0:T(8,128)(2,1)} async-done(((bf16[512,768]{1,0:T(8,128)(2,1)}), bf16[2048,768]{1,0:T(8,128)(2,1)}) %all-gather.10.cloned.1.call-update) | async-done | bytes 3145744 | tf_op jit(solution)/shard_map/all_gather | solution.py:234
  80.7 27.5 %all-gather.8.cloned.1.call-done = bf16[2048,768]{1,0:T(8,128)(2,1)} async-done(((bf16[512,768]{1,0:T(8,128)(2,1)}), bf16[2048,768]{1,0:T(8,128)(2,1)}) %all-gather.8.cloned.1.call-update) | async-done | bytes 3145744 | tf_op jit(solution)/shard_map/all_gather | solution.py:235
  113.0 488.4 %while.34 = (s32[]{:T(128)}, bf16[3,512,4,64]{1,3,2,0:T(8,128)(2,1)}, f32[3,1,4,512]{3,2,1,0:T(4,128)}, bf16[3,2048,4,64]{1,3,2,0:T(8,128)(2,1)}, bf16[3,512,4,6...) while((s32[]{:T(128)}, ...), condition=%wide.region_4.5_spmd, body=%wide.region_1.4_spmd.sunk | while | flops 1107425280 | bytes 258697328 | solution.py:89
  123.8 23.4 %copy.60 = f32[1,4,512,2560]{3,1,2,0:T(4,128)S(1)} copy(f32[1,4,512,2560]{3,2,1,0:T(8,128)} %broadcast_bitcast_fusion.4) | data formatting | bytes 41943040 | tf_op jit(solution)/shard_map/while
  155.5 59.2 %reshape.345 = f32[5240832]{0:T(1024)} reshape(f32[4,1310208]{1,0:T(4,128)} %slice.88) | data formatting | bytes 41926656 | tf_op jit(solution)/shard_map/while
  214.7 29.6 %reshape.346 = f32[4,512,2559]{2,1,0:T(8,128)} reshape(f32[5240832]{0:T(1024)} %reshape.345) | data formatting | bytes 41926656 | tf_op jit(solution)/shard_map/while/body/eval_jaxpr/while/body/eval_jaxpr/reshape | solution.py:26
  244.3 12.4 fusion.194
  284.7 23.4 %copy.60 = f32[1,4,512,2560]{3,1,2,0:T(4,128)S(1)} copy(f32[1,4,512,2560]{3,2,1,0:T(8,128)} %broadcast_bitcast_fusion.4) | data formatting | bytes 41943040 | tf_op jit(solution)/shard_map/while
  316.6 58.9 %reshape.345 = f32[5240832]{0:T(1024)} reshape(f32[4,1310208]{1,0:T(4,128)} %slice.88) | data formatting | bytes 41926656 | tf_op jit(solution)/shard_map/while
  375.4 29.7 %reshape.346 = f32[4,512,2559]{2,1,0:T(8,128)} reshape(f32[5240832]{0:T(1024)} %reshape.345) | data formatting | bytes 41926656 | tf_op jit(solution)/shard_map/while/body/eval_jaxpr/while/body/eval_jaxpr/reshape | solution.py:26
  405.1 12.4 fusion.194
  445.7 23.4 %copy.60 = f32[1,4,512,2560]{3,1,2,0:T(4,128)S(1)} copy(f32[1,4,512,2560]{3,2,1,0:T(8,128)} %broadcast_bitcast_fusion.4) | data formatting | bytes 41943040 | tf_op jit(solution)/shard_map/while
  477.3 58.9 %reshape.345 = f32[5240832]{0:T(1024)} reshape(f32[4,1310208]{1,0:T(4,128)} %slice.88) | data formatting | bytes 41926656 | tf_op jit(solution)/shard_map/while
  536.2 29.8 %reshape.346 = f32[4,512,2559]{2,1,0:T(8,128)} reshape(f32[5240832]{0:T(1024)} %reshape.345) | data formatting | bytes 41926656 | tf_op jit(solution)/shard_map/while/body/eval_jaxpr/while/body/eval_jaxpr/reshape | solution.py:26
  566.1 12.4 fusion.194
  628.3 24.8 %all-to-all-done = bf16[8,128,768]{2,1,0:T(8,128)(2,1)} async-done(((bf16[8,128,768]{2,1,0:T(8,128)(2,1)}), bf16[8,128,768]{2,1,0:T(8,128)(2,1)}, u32[]{:S(2)}, u32[]{:S(2)}) %all-to-all-start) | async-done | bytes 1572896 | tf_op jit(solution)/shard_map/all_to_all | solution.py:270
  680.3 14.0 all-to-all-done.2
  698.9 15.3 fusion.71
  746.6 29.8 %all-to-all-done.3 = bf16[8,128,768]{2,1,0:T(8,128)(2,1)} async-done(((bf16[8,128,768]{2,1,0:T(8,128)(2,1)}), bf16[8,128,768]{2,1,0:T(8,128)(2,1)}, u32[]{:S(2)}, u32[]{:S(2)}) %all-to-all-start.3) | async-done | bytes 1572896 | tf_op jit(solution)/shard_map/all_to_all | solution.py:305
  791.0 790.9 %while.35 = (s32[]{:T(128)}, bf16[3,512,4,64]{1,3,2,0:T(8,128)(2,1)}, bf16[3,2048,4,64]{1,3,2,0:T(8,128)(2,1)}, bf16[3,2048,4,64]{1,3,2,0:T(8,128)(2,1)}, f32[3,...) while((s32[]{:T(128)}, ...), condition=%wide.region_19.20_spmd, body=%wide.region_16.19_spmd.sunk | while | flops 2732183552 | bytes 655389952 | solution.py:162
  802.9 23.4 %copy.62 = f32[1,4,512,2560]{3,1,2,0:T(4,128)S(1)} copy(f32[1,4,512,2560]{3,2,1,0:T(8,128)} %broadcast_bitcast_fusion.5) | data formatting | bytes 41943040 | tf_op jit(solution)/shard_map/while
  834.5 58.6 %reshape.347 = f32[5240832]{0:T(1024)} reshape(f32[4,1310208]{1,0:T(4,128)} %slice.91) | data formatting | bytes 41926656 | tf_op jit(solution)/shard_map/while
  893.2 29.9 %reshape.348 = f32[4,512,2559]{2,1,0:T(8,128)} reshape(f32[5240832]{0:T(1024)} %reshape.347) | data formatting | bytes 41926656 | tf_op jit(solution)/shard_map/while/body/eval_jaxpr/while/body/eval_jaxpr/reshape | solution.py:26
  943.1 11.8 subtract_multiply_fusion.2
  977.8 30.2 %reshape.349 = f32[5240832]{0:T(1024)} reshape(f32[4,512,2559]{2,1,0:T(8,128)} %pad.62) | data formatting | bytes 41926656 | tf_op jit(solution)/shard_map/while
  1007.9 25.5 %reshape.350 = f32[4,1310208]{1,0:T(4,128)} reshape(f32[5240832]{0:T(1024)} %reshape.349) | data formatting | bytes 41926656 | tf_op jit(solution)/shard_map/while/body/eval_jaxpr/while/body/eval_jaxpr/reshape | solution.py:34
  1033.4 11.3 pad.63
  1063.1 23.4 %copy.62 = f32[1,4,512,2560]{3,1,2,0:T(4,128)S(1)} copy(f32[1,4,512,2560]{3,2,1,0:T(8,128)} %broadcast_bitcast_fusion.5) | data formatting | bytes 41943040 | tf_op jit(solution)/shard_map/while
  1094.8 58.6 %reshape.347 = f32[5240832]{0:T(1024)} reshape(f32[4,1310208]{1,0:T(4,128)} %slice.91) | data formatting | bytes 41926656 | tf_op jit(solution)/shard_map/while
  1153.4 29.9 %reshape.348 = f32[4,512,2559]{2,1,0:T(8,128)} reshape(f32[5240832]{0:T(1024)} %reshape.347) | data formatting | bytes 41926656 | tf_op jit(solution)/shard_map/while/body/eval_jaxpr/while/body/eval_jaxpr/reshape | solution.py:26
  1203.4 11.8 subtract_multiply_fusion.2
  1238.1 30.2 %reshape.349 = f32[5240832]{0:T(1024)} reshape(f32[4,512,2559]{2,1,0:T(8,128)} %pad.62) | data formatting | bytes 41926656 | tf_op jit(solution)/shard_map/while
  1268.3 25.5 %reshape.350 = f32[4,1310208]{1,0:T(4,128)} reshape(f32[5240832]{0:T(1024)} %reshape.349) | data formatting | bytes 41926656 | tf_op jit(solution)/shard_map/while/body/eval_jaxpr/while/body/eval_jaxpr/reshape | solution.py:34
  1293.8 11.3 pad.63
  1323.5 23.4 %copy.62 = f32[1,4,512,2560]{3,1,2,0:T(4,128)S(1)} copy(f32[1,4,512,2560]{3,2,1,0:T(8,128)} %broadcast_bitcast_fusion.5) | data formatting | bytes 41943040 | tf_op jit(solution)/shard_map/while
  1355.2 58.6 %reshape.347 = f32[5240832]{0:T(1024)} reshape(f32[4,1310208]{1,0:T(4,128)} %slice.91) | data formatting | bytes 41926656 | tf_op jit(solution)/shard_map/while
  1413.8 29.9 %reshape.348 = f32[4,512,2559]{2,1,0:T(8,128)} reshape(f32[5240832]{0:T(1024)} %reshape.347) | data formatting | bytes 41926656 | tf_op jit(solution)/shard_map/while/body/eval_jaxpr/while/body/eval_jaxpr/reshape | solution.py:26
  1463.7 11.8 subtract_multiply_fusion.2
  1498.4 30.2 %reshape.349 = f32[5240832]{0:T(1024)} reshape(f32[4,512,2559]{2,1,0:T(8,128)} %pad.62) | data formatting | bytes 41926656 | tf_op jit(solution)/shard_map/while
  1528.6 25.5 %reshape.350 = f32[4,1310208]{1,0:T(4,128)} reshape(f32[5240832]{0:T(1024)} %reshape.349) | data formatting | bytes 41926656 | tf_op jit(solution)/shard_map/while/body/eval_jaxpr/while/body/eval_jaxpr/reshape | solution.py:34
  1554.1 11.3 pad.63
  1582.5 12.1 fusion.97
  1618.5 40.5 %reduce-scatter.10.cloned.1.call-done = bf16[512,768]{0,1:T(8,128)(2,1)} async-done(((bf16[2048,768]{0,1:T(8,128)(2,1)}), bf16[512,768]{0,1:T(8,128)(2,1)}) %reduce-scatter.10.cloned.1.call-update) | async-done | bytes 786448 | tf_op jit(solution)/shard_map/reduce_scatter | solution.py:346
  1674.4 40.6 %all-reduce.9 = (f32[768]{0:T(1024)S(1)}, f32[32,12]{0,1:T(8,128)}, f32[768]{0:T(1024)S(1)}, f32[768,8]{0,1:T(8,128)S(1)}) all-reduce(f32[768]{0:T(1024)S(1)} %get-tuple-element.446, f32[32,12]{0,1:T(8,128)S(1)} %fusion.135, f32[768]{0:T(1024)S(1)} %copy-done.32, ...), channel_id=4, replica_groups=mesh['expert'=8,'wshard'=4] {'expert','wshard'}, use_global_device_ids=true, to_apply=%region_24.25.clone | all-reduce | flops 8064 | bytes 64512
  1723.3 37.2 %reduce-scatter.16.cloned.1.call-done = bf16[1,768,768]{2,1,0:T(8,128)(2,1)} async-done(((bf16[1,768,3072]{2,1,0:T(8,128)(2,1)}), bf16[1,768,768]{2,1,0:T(8,128)(2,1)}) %reduce-scatter.16.cloned.1.call-update) | async-done | bytes 1179664 | tf_op jit(solution)/shard_map/reduce_scatter | solution.py:297
  1763.3 102.0 %reduce-scatter.14.cloned.1.call-done = f32[24,768]{1,0:T(8,128)} async-done(((f32[768,768]{1,0:T(8,128)}), f32[24,768]{1,0:T(8,128)}) %reduce-scatter.14.cloned.1.call-update) | async-done | bytes 73744 | tf_op jit(solution)/shard_map/reduce_scatter | solution.py:366
  1865.3 125.3 %reduce-scatter.12.cloned.1.call-done = f32[24,2304]{1,0:T(8,128)} async-done(((f32[768,2304]{1,0:T(8,128)}), f32[24,2304]{1,0:T(8,128)}) %reduce-scatter.12.cloned.1.call-update) | async-done | bytes 221200 | tf_op jit(solution)/shard_map/reduce_scatter | solution.py:365
  (283 shorter events, 505.0 us)
Async XLA Ops:
  7.2 45.6 %copy-start = (bf16[32,12]{0,1:T(8,128)(2,1)S(1)}, bf16[32,12]{0,1:T(8,128)(2,1)}, u32[]{:S(2)}) copy-start(bf16[32,12]{0,1:T(8,128)(2,1)} %param.20) | copy-start | bytes 2308
  7.2 35.9 %all-gather.6.cloned.1.call-start = ((), (), s32[]{:S(2)}) async-start(), calls=%async_computation.10 | async-start | bytes 4423680 | tf_op jit(solution)/shard_map/all_gather | solution.py:218
  7.9 69.5 %all-gather.10.cloned.1.call-start = ((), (), s32[]{:S(2)}) async-start(), calls=%async_computation.12 | async-start | bytes 3932160 | tf_op jit(solution)/shard_map/all_gather | solution.py:234
  19.9 23.2 %copy-start.33 = (f32[768]{0:T(1024)}, f32[768]{0:T(1024)S(1)}, u32[]{:S(2)}) copy-start(f32[768]{0:T(1024)S(1)} %convert_element_type.155) | copy-start | bytes 9220
  21.9 21.2 %copy-start.36 = (f32[512]{0:T(512)}, f32[512]{0:T(512)S(1)}, u32[]{:S(2)}) copy-start(f32[512]{0:T(512)S(1)} %get-tuple-element.506) | copy-start | bytes 6148
  48.8 59.4 %all-gather.8.cloned.1.call-start = ((), (), s32[]{:S(2)}) async-start(), calls=%async_computation.11 | async-start | bytes 3932160 | tf_op jit(solution)/shard_map/all_gather | solution.py:235
  49.5 551.9 %all-gather.12.cloned.1.call-start = ((), (), s32[]{:S(2)}) async-start(), calls=%async_computation.13 | async-start | bytes 1474560 | tf_op jit(solution)/shard_map/all_gather | solution.py:219
  605.1 10.5 copy-start.39
  609.8 13.9 copy-start.20
  609.9 43.3 %all-to-all-start = ((bf16[8,128,768]{2,1,0:T(8,128)(2,1)}), bf16[8,128,768]{2,1,0:T(8,128)(2,1)}, u32[]{:S(2)}, u32[]{:S(2)}) async-start(bf16[8,128,768]{2,1,0:T(8,128)(2,1)} %bitcast.291), calls=%async_computation | async-start | bytes 3145728 | tf_op jit(solution)/shard_map/all_to_all | solution.py:270
  623.7 157.4 %copy-start.16 = (f32[512,8]{0,1:T(8,128)}, f32[512,8]{0,1:T(8,128)S(1)}, u32[]{:S(2)}) copy-start(f32[512,8]{0,1:T(8,128)S(1)} %get-tuple-element.512) | copy-start | bytes 49156
  623.7 157.4 %copy-start.24 = (f32[512]{0:T(512)}, f32[512]{0:T(512)S(1)}, u32[]{:S(2)}) copy-start(f32[512]{0:T(512)S(1)} %get-tuple-element.511) | copy-start | bytes 6148
  623.8 157.4 %copy-start.28 = (f32[512]{0:T(512)}, f32[512]{0:T(512)S(1)}, u32[]{:S(2)}) copy-start(f32[512]{0:T(512)S(1)} %fusion.146) | copy-start | bytes 6148
  653.1 41.2 %all-to-all-start.2 = ((bf16[8,128,768]{2,1,0:T(8,128)(2,1)}), bf16[8,128,768]{2,1,0:T(8,128)(2,1)}, u32[]{:S(2)}, u32[]{:S(2)}) async-start(bf16[8,128,768]{2,1,0:T(8,128)(2,1)} %bitcast.292), calls=%async_computation.2 | async-start | bytes 3145728 | tf_op jit(solution)/shard_map/all_to_all | solution.py:290
  694.3 41.2 %all-to-all-start.1 = ((bf16[8,128,768]{2,1,0:T(8,128)(2,1)}), bf16[8,128,768]{2,1,0:T(8,128)(2,1)}, u32[]{:S(2)}, u32[]{:S(2)}) async-start(bf16[8,128,768]{2,1,0:T(8,128)(2,1)} %fusion.102), calls=%async_computation.1 | async-start | bytes 3145728 | tf_op jit(solution)/shard_map/all_to_all | solution.py:275
  735.5 40.9 %all-to-all-start.3 = ((bf16[8,128,768]{2,1,0:T(8,128)(2,1)}), bf16[8,128,768]{2,1,0:T(8,128)(2,1)}, u32[]{:S(2)}, u32[]{:S(2)}) async-start(bf16[8,128,768]{2,1,0:T(8,128)(2,1)} %fusion.107), calls=%async_computation.3 | async-start | bytes 3145728 | tf_op jit(solution)/shard_map/all_to_all | solution.py:305
  739.8 878.6 %reduce-scatter.8.cloned.1.call-start = ((), (), s32[]{:S(2)}) async-start(), calls=%async_computation.14 | async-start | bytes 3932160 | tf_op jit(solution)/shard_map/reduce_scatter | solution.py:343
  746.6 34.6 %copy-start.26 = (f32[512]{0:T(512)}, f32[512]{0:T(512)S(1)}, u32[]{:S(2)}) copy-start(f32[512]{0:T(512)S(1)} %fusion.116) | copy-start | bytes 6148
  746.6 34.6 %copy-start.30 = (f32[512]{0:T(512)}, f32[512]{0:T(512)S(1)}, u32[]{:S(2)}) copy-start(f32[512]{0:T(512)S(1)} %mul.321) | copy-start | bytes 6148
  791.6 11.3 copy-start.3
  893.2 29.9 %copy-start.5 = (bf16[3,512,4,64]{1,3,2,0:T(8,128)(2,1)S(1)}, bf16[3,512,4,64]{1,3,2,0:T(8,128)(2,1)}, u32[]{:S(2)}) copy-start(bf16[3,512,4,64]{1,3,2,0:T(8,128)(2,1)} %get-tuple-element.727) | copy-start | bytes 2359300 | tf_op jit(solution)/shard_map/while
  923.1 9.1 copy-start.7
  943.1 11.8 copy-start.41
  954.9 10.9 copy-start.2
  1044.7 6.6 copy-start.4
  1051.8 11.3 copy-start.3
  1153.4 29.9 %copy-start.5 = (bf16[3,512,4,64]{1,3,2,0:T(8,128)(2,1)S(1)}, bf16[3,512,4,64]{1,3,2,0:T(8,128)(2,1)}, u32[]{:S(2)}) copy-start(bf16[3,512,4,64]{1,3,2,0:T(8,128)(2,1)} %get-tuple-element.727) | copy-start | bytes 2359300 | tf_op jit(solution)/shard_map/while
  1183.3 9.1 copy-start.7
  1203.4 11.8 copy-start.41
  1215.2 10.9 copy-start.2
  1305.1 6.6 copy-start.4
  1312.2 11.3 copy-start.3
  1413.8 29.9 %copy-start.5 = (bf16[3,512,4,64]{1,3,2,0:T(8,128)(2,1)S(1)}, bf16[3,512,4,64]{1,3,2,0:T(8,128)(2,1)}, u32[]{:S(2)}) copy-start(bf16[3,512,4,64]{1,3,2,0:T(8,128)(2,1)} %get-tuple-element.727) | copy-start | bytes 2359300 | tf_op jit(solution)/shard_map/while
  1443.7 9.1 copy-start.7
  1463.7 11.8 copy-start.41
  1475.5 10.9 copy-start.2
  1565.4 6.6 copy-start.4
  1581.9 77.1 %reduce-scatter.10.cloned.1.call-start = ((), (), s32[]{:S(2)}) async-start(), calls=%async_computation.15 | async-start | bytes 3932160 | tf_op jit(solution)/shard_map/reduce_scatter | solution.py:346
  1582.5 137.6 %reduce-scatter.18.cloned.1.call-start = ((), (), s32[]{:S(2)}) async-start(), calls=%async_computation.19 | async-start | bytes 5898240 | tf_op jit(solution)/shard_map/reduce_scatter | solution.py:300
  1594.6 165.9 %reduce-scatter.16.cloned.1.call-start = ((), (), s32[]{:S(2)}) async-start(), calls=%async_computation.18 | async-start | bytes 5898240 | tf_op jit(solution)/shard_map/reduce_scatter | solution.py:297
  1603.9 55.1 %copy-start.14 = (bf16[512,768]{1,0:T(8,128)(2,1)S(1)}, bf16[512,768]{1,0:T(8,128)(2,1)}, u32[]{:S(2)}) copy-start(bf16[512,768]{1,0:T(8,128)(2,1)} %param.16) | copy-start | bytes 2359300
  1603.9 55.1 %copy-start.34 = (f32[768]{0:T(1024)S(1)}, f32[768]{0:T(1024)}, u32[]{:S(2)}) copy-start(f32[768]{0:T(1024)} %copy-done.33) | copy-start | bytes 9220
  1603.9 55.1 %copy-start.37 = (f32[512]{0:T(512)S(1)}, f32[512]{0:T(512)}, u32[]{:S(2)}) copy-start(f32[512]{0:T(512)} %copy-done.36) | copy-start | bytes 6148
  1603.9 261.4 %reduce-scatter.14.cloned.1.call-start = ((), (), s32[]{:S(2)}) async-start(), calls=%async_computation.17 | async-start | bytes 2433024 | tf_op jit(solution)/shard_map/reduce_scatter | solution.py:366
  1607.7 382.9 %reduce-scatter.12.cloned.1.call-start = ((), (), s32[]{:S(2)}) async-start(), calls=%async_computation.16 | async-start | bytes 7299072 | tf_op jit(solution)/shard_map/reduce_scatter | solution.py:365
  1667.5 6.9 copy-start.32
  1667.5 49.3 %copy-start.35 = (f32[512]{0:T(512)S(1)}, f32[512]{0:T(512)}, u32[]{:S(2)}) copy-start(f32[512]{0:T(512)} %get-tuple-element.505) | copy-start | bytes 6148
  1716.8 273.8 %copy-start.1 = (bf16[32,12]{0,1:T(8,128)(2,1)S(1)}, bf16[32,12]{0,1:T(8,128)(2,1)}, u32[]{:S(2)}) copy-start(bf16[32,12]{0,1:T(8,128)(2,1)} %param.20) | copy-start | bytes 2308
  (25 other events, 60.3 us)
Sparse Core Ops, SparseCore 0:
  9.6 33.4 all-gather.5
  48.9 28.5 all-gather.9
  79.6 28.5 all-gather.7
  109.6 17.4 all-gather.11
  1582.0 36.3 reduce-scatter.7
  1621.0 37.9 reduce-scatter.9
  1661.5 48.3 reduce-scatter.17
  1712.7 47.7 reduce-scatter.15
  1766.3 98.9 reduce-scatter.13
  1872.4 118.1 reduce-scatter.11
where the time goes:
time: 2000 us
  local copies, waits for them, and re-layouts  1070 us (54%)
  waiting for transfers between devices  468 us (23%)
  matrix products  250 us (12%)
  other arithmetic  106 us (5%)
  blocking collectives  54.1 us (3%)
    while x63, local copies, waits for them, and re-layouts  648 us
    reshape x6, local copies, waits for them, and re-layouts, expand_offsets(): repeated.reshape(head_count, row_count, span - 1)[:, :, row_count - 1:]  179 us
    reduce_scatter x1, waiting for transfers between devices, local(): lax.psum_scatter(grad_attn_in, ('expert', 'wshard'), scatter_dimension=0,...  125 us
    reduce_scatter x1, waiting for transfers between devices, local(): lax.psum_scatter(grad_attn_out, ('expert', 'wshard'), scatter_dimension=0...  102 us
    reshape x3, local copies, waits for them, and re-layouts, fold_offsets(): placed.reshape(head_count, row_count * (span - 1))  76.5 us
    dot_general x6, matrix products, block_scores(): jnp.einsum('qhd,khd->hqk', query_heads, key_heads, preferred_element_type...  64.5 us
    slice x6, local copies, waits for them, and re-layouts, expand_offsets(): repeated = jnp.tile(padded, (1, row_count))[:, :row_count * (span - 1)]  49.6 us
    unnamed x2, blocking collectives  48.9 us
  transfers between devices with their start and end apart: 14, of which 12 were waited for; matrix products, arithmetic and copies ran while one was open for 30% of the time, Pallas kernels for 0%

commit v1 on v0

v1 whole, which is shorter than its diff:
```python
import functools
import math

import jax
import jax.numpy as jnp
from jax import lax
from jax.experimental import pallas as pl
from jax.experimental.pallas import tpu as pltpu
from jax.sharding import PartitionSpec as P

epsilon = 1e-06
highest = lax.Precision.HIGHEST
f32 = jnp.float32
bf16 = jnp.bfloat16
LOG2E = math.log2(math.e)
LANES = 128
BLOCK = 256


def rms_scale(values):
    return lax.rsqrt(jnp.mean(values * values, axis=-1, keepdims=True) + epsilon)


def norm_back(grad_normed, values, scale, gain):
    scaled = grad_normed * gain
    inner_mean = jnp.mean(scaled * values, axis=-1, keepdims=True)
    grad_values = scale * scaled - values * (scale * scale * scale) * inner_mean
    return (grad_values, jnp.sum(grad_normed * values * scale, axis=0))


def build_bias(offsets, bias_ref):
    chunks = offsets.shape[0]
    rows = jnp.broadcast_to(offsets[:, None, :], (chunks, 8, LANES)).reshape(chunks * 8, LANES)
    sub = lax.broadcasted_iota(jnp.int32, (chunks * 8, LANES), 0) % 8
    for bit in (1, 2, 4):
        rows = jnp.where((sub & bit) != 0, pltpu.roll(rows, bit, 1), rows)
    lane = lax.broadcasted_iota(jnp.int32, (8, LANES), 1)
    sub8 = lax.broadcasted_iota(jnp.int32, (8, LANES), 0)
    for part in range(LANES // 8):
        turned = pltpu.roll(rows, 8 * part, 1) if part else rows
        upper = lane >= sub8 + 8 * part
        for tile in range(chunks - 1):
            chunk = chunks - 1 - tile
            bias_ref[tile * LANES + 8 * part : tile * LANES + 8 * part + 8, :] = jnp.where(
                upper, turned[chunk * 8 : chunk * 8 + 8], turned[chunk * 8 - 8 : chunk * 8]
            )


def fold_bias(grad_ref, chunks):
    lane = lax.broadcasted_iota(jnp.int32, (LANES, LANES), 1)
    sub = lax.broadcasted_iota(jnp.int32, (LANES, LANES), 0)
    upper = lane >= sub
    pieces = []
    for chunk in range(chunks):
        total = None
        if chunk >= 1:
            start = (chunks - 1 - chunk) * LANES
            total = jnp.where(upper, grad_ref[start : start + LANES, :], 0.0)
        if chunk <= chunks - 2:
            start = (chunks - 2 - chunk) * LANES
            lower = jnp.where(upper, 0.0, grad_ref[start : start + LANES, :])
            total = lower if total is None else total + lower
        half = LANES // 2
        while half >= 8:
            total = total[:half] + pltpu.roll(total[half:], LANES - half, 1)
            half //= 2
        pieces.append(total)
    stacked = jnp.concatenate(pieces, axis=0)
    sub8 = lax.broadcasted_iota(jnp.int32, (chunks * 8, LANES), 0) % 8
    for bit in (1, 2, 4):
        stacked = jnp.where((sub8 & bit) != 0, pltpu.roll(stacked, LANES - bit, 1), stacked)
    return jnp.sum(stacked.reshape(chunks, 8, LANES), axis=1)


def split_scaled(query):
    scaled = query.astype(f32) * (0.125 * LOG2E)
    high = scaled.astype(bf16)
    low = (scaled - high.astype(f32)).astype(bf16)
    return jnp.concatenate([high, low], axis=0)


def strips(bias_ref, tiles, first, start, count):
    parts = []
    for index in range(count):
        row = (tiles - 1 - (first + index)) * LANES + start
        parts.append(bias_ref[pl.ds(pl.multiple_of(row, LANES), BLOCK), :])
    return jnp.concatenate(parts, axis=1)


def forward_kernel(
    offset_ref, query_ref, key_ref, value_ref, mixed_ref, log_ref, bias_ref, key2_ref, value_aug_ref, score_ref
):
    size, length = query_ref.shape
    tiles = length // LANES
    blocks = length // BLOCK
    across = BLOCK // LANES
    build_bias(offset_ref[0] * LOG2E, bias_ref)
    keys = key_ref[...].astype(f32).T.astype(bf16)
    key2_ref[...] = jnp.concatenate([keys, keys], axis=1)
    value_aug_ref[:size, :] = value_ref[...]
    extra = lax.broadcasted_iota(jnp.int32, (16, length), 0)
    value_aug_ref[size:, :] = jnp.where(extra == 0, 1.0, 0.0).astype(bf16)

    def one_block(block, carry):
        columns = pl.ds(pl.multiple_of(block * BLOCK, BLOCK), BLOCK)
        query2 = split_scaled(query_ref[:, columns])
        top = jnp.full((1, BLOCK), -jnp.inf, f32)
        for chunk in range(blocks):
            start = chunk * BLOCK
            scores = jnp.dot(key2_ref[start : start + BLOCK, :], query2, preferred_element_type=f32)
            scores = scores + strips(bias_ref, tiles, block * across, start, across)
            score_ref[start : start + BLOCK, :] = scores
            top = jnp.maximum(top, jnp.max(scores, axis=0, keepdims=True))
        total = jnp.zeros((size + 16, BLOCK), f32)
        for chunk in range(blocks):
            start = chunk * BLOCK
            weights = jnp.exp2(score_ref[start : start + BLOCK, :] - top).astype(bf16)
            total = total + jnp.dot(
                value_aug_ref[:, start : start + BLOCK], weights, preferred_element_type=f32
            )
        row_total = total[size : size + 1]
        mixed_ref[:, columns] = (total[:size] / row_total).astype(bf16)
        log_ref[0, :, columns] = top + jnp.log2(row_total)
        return carry

    lax.fori_loop(0, blocks, one_block, 0)


def backward_kernel(
    offset_ref,
    query_ref,
    key_ref,
    value_ref,
    grad_ref,
    mixed_ref,
    log_ref,
    dquery_ref,
    dkey_ref,
    dvalue_ref,
    doffset_ref,
    bias_ref,
    dbias_ref,
    query2_ref,
    query_rows_ref,
    grad_rows_ref,
    key2_ref,
    value_rows_ref,
    delta_ref,
    weight_ref,
    score_ref,
    dquery_acc_ref,
):
    size, length = query_ref.shape
    tiles = length // LANES
    blocks = length // BLOCK
    across = BLOCK // LANES
    build_bias(offset_ref[0] * LOG2E, bias_ref)
    dbias_ref[...] = jnp.zeros_like(dbias_ref)
    query2_ref[...] = split_scaled(query_ref[...])
    query_rows_ref[...] = query_ref[...].astype(f32).T.astype(bf16)
    grad = grad_ref[...].astype(f32)
    grad_rows_ref[...] = grad.T.astype(bf16)
    keys = key_ref[...].astype(f32).T.astype(bf16)
    key2_ref[...] = jnp.concatenate([keys, keys], axis=1)
    value_rows_ref[...] = value_ref[...].astype(f32).T.astype(bf16)
    delta_ref[...] = jnp.sum(grad * mixed_ref[...].astype(f32), axis=0, keepdims=True)
    dquery_acc_ref[...] = jnp.zeros_like(dquery_acc_ref)

    def one_chunk(chunk, carry):
        start = pl.multiple_of(chunk * BLOCK, BLOCK)
        rows = pl.ds(start, BLOCK)
        for block in range(blocks):
            columns = slice(block * BLOCK, (block + 1) * BLOCK)
            scores = jnp.dot(key2_ref[rows, :], query2_ref[:, columns], preferred_element_type=f32)
            scores = scores + strips(bias_ref, tiles, block * across, start, across)
            weights = jnp.exp2(scores - log_ref[0, :, columns])
            weight_ref[:, columns] = weights.astype(bf16)
            dweights = jnp.dot(value_rows_ref[rows, :], grad_ref[:, columns], preferred_element_type=f32)
            dscores = weights * (dweights - delta_ref[:, columns])
            for index in range(across):
                row = (tiles - 1 - (block * across + index)) * LANES + start
                place = pl.ds(pl.multiple_of(row, LANES), BLOCK)
                dbias_ref[place, :] += dscores[:, index * LANES : (index + 1) * LANES]
            low = dscores.astype(bf16)
            score_ref[:, columns] = low
            dquery_acc_ref[:, columns] += jnp.dot(key_ref[:, rows], low, preferred_element_type=f32)
        dvalue = jnp.dot(weight_ref[...], grad_rows_ref[...], preferred_element_type=f32)
        dkey = jnp.dot(score_ref[...], query_rows_ref[...], preferred_element_type=f32) * 0.125
        dvalue_ref[:, rows] = dvalue.T.astype(bf16)
        dkey_ref[:, rows] = dkey.T.astype(bf16)
        return carry

    lax.fori_loop(0, blocks, one_chunk, 0)
    dquery_ref[...] = (dquery_acc_ref[...] * 0.125).astype(bf16)
    doffset_ref[0] = fold_bias(dbias_ref, offset_ref.shape[1])


def attention_forward(offsets, qkv, heads):
    columns, length = qkv.shape
    size = columns // (3 * heads)
    chunks = offsets.shape[1]
    elements = heads * length * length
    return pl.pallas_call(
        forward_kernel,
        grid=(heads,),
        in_specs=[
            pl.BlockSpec((1, chunks, LANES), lambda h: (h, 0, 0)),
            pl.BlockSpec((size, length), lambda h: (h, 0)),
            pl.BlockSpec((size, length), lambda h: (heads + h, 0)),
            pl.BlockSpec((size, length), lambda h: (2 * heads + h, 0)),
        ],
        out_specs=[
            pl.BlockSpec((size, length), lambda h: (h, 0)),
            pl.BlockSpec((1, 1, length), lambda h: (h, 0, 0)),
        ],
        out_shape=[
            jax.ShapeDtypeStruct((heads * size, length), bf16),
            jax.ShapeDtypeStruct((heads, 1, length), f32),
        ],
        scratch_shapes=[
            pltpu.VMEM(((chunks - 1) * LANES, LANES), f32),
            pltpu.VMEM((length, 2 * size), bf16),
            pltpu.VMEM((size + 16, length), bf16),
            pltpu.VMEM((length, BLOCK), f32),
        ],
        compiler_params=pltpu.CompilerParams(vmem_limit_bytes=48 * 1024 * 1024),
        cost_estimate=pl.CostEstimate(
            flops=elements * 64 * 4 * 4, bytes_accessed=8 * 1024 * 1024, transcendentals=elements
        ),
    )(offsets, qkv, qkv, qkv)


def attention_backward(offsets, qkv, grad, mixed, logs, heads):
    columns, length = qkv.shape
    size = columns // (3 * heads)
    chunks = offsets.shape[1]
    elements = heads * length * length
    rows = pl.BlockSpec((size, length), lambda h: (h, 0))
    return pl.pallas_call(
        backward_kernel,
        grid=(heads,),
        in_specs=[
            pl.BlockSpec((1, chunks, LANES), lambda h: (h, 0, 0)),
            rows,
            pl.BlockSpec((size, length), lambda h: (heads + h, 0)),
            pl.BlockSpec((size, length), lambda h: (2 * heads + h, 0)),
            rows,
            rows,
            pl.BlockSpec((1, 1, length), lambda h: (h, 0, 0)),
        ],
        out_specs=[rows, rows, rows, pl.BlockSpec((1, chunks, LANES), lambda h: (h, 0, 0))],
        out_shape=[jax.ShapeDtypeStruct((heads * size, length), bf16)] * 3
        + [jax.ShapeDtypeStruct((heads, chunks, LANES), f32)],
        scratch_shapes=[
            pltpu.VMEM(((chunks - 1) * LANES, LANES), f32),
            pltpu.VMEM(((chunks - 1) * LANES, LANES), f32),
            pltpu.VMEM((2 * size, length), bf16),
            pltpu.VMEM((length, size), bf16),
            pltpu.VMEM((length, size), bf16),
            pltpu.VMEM((length, 2 * size), bf16),
            pltpu.VMEM((length, size), bf16),
            pltpu.VMEM((1, length), f32),
            pltpu.VMEM((BLOCK, length), bf16),
            pltpu.VMEM((BLOCK, length), bf16),
            pltpu.VMEM((size, length), f32),
        ],
        compiler_params=pltpu.CompilerParams(vmem_limit_bytes=48 * 1024 * 1024),
        cost_estimate=pl.CostEstimate(
            flops=elements * 64 * 10 * 4, bytes_accessed=12 * 1024 * 1024, transcendentals=elements
        ),
    )(offsets, qkv, qkv, qkv, grad, mixed, logs)


def gelu_parts(inner):
    root = math.sqrt(2.0 / math.pi)
    bent = jnp.tanh(root * (inner + 0.044715 * (inner * inner * inner)))
    hidden = 0.5 * inner * (1.0 + bent)
    slope = 0.5 * (1.0 + bent) + 0.5 * inner * (1.0 - bent * bent) * (
        root * (1.0 + 3 * 0.044715 * (inner * inner))
    )
    return hidden, slope


def exchange(rows, axis):
    return lax.all_to_all(rows, axis, split_axis=0, concat_axis=0, tiled=True)


def local(
    tokens,
    attn_norm,
    attn_in,
    attn_out,
    rel_bias,
    buckets,
    ffn_norm,
    router,
    routes,
    expert_in,
    expert_out,
    cotangent,
):
    shards = lax.axis_size("wshard")
    here = lax.axis_index("wshard")
    owner = lax.axis_index("expert")
    rows, width = tokens.shape
    length = rows * shards
    bucket_count, head_total = rel_bias.shape
    heads = head_total // shards
    part = width // shards
    experts = router.shape[1]
    capacity = max(2, 2 * rows // experts)

    small = jnp.concatenate([attn_norm, ffn_norm, router.T.reshape(-1)])
    small_rows = -(-small.shape[0] // (16 * width)) * 16
    small = jnp.pad(small, (0, small_rows * width - small.shape[0])).reshape(small_rows, width)
    gathered = lax.all_gather(jnp.concatenate([tokens, small], axis=0), "wshard", axis=0)
    seq_tokens = gathered[:, :rows].reshape(length, width).astype(f32)
    small_all = gathered[:, rows:].reshape(shards, -1)
    gain_a = small_all[:, :part].reshape(width).astype(f32)
    gain_f = small_all[:, part : 2 * part].reshape(width).astype(f32)
    full_router = (
        small_all[:, 2 * part : (2 + experts) * part]
        .reshape(shards, experts, part)
        .transpose(1, 0, 2)
        .reshape(experts, width)
    )

    sorted_in = attn_in.reshape(part, 3, shards, part).transpose(2, 0, 1, 3).reshape(shards, part, 3 * part)
    own_in = exchange(sorted_in, "wshard").reshape(width, 3 * part)

    seq_normed = (seq_tokens * rms_scale(seq_tokens) * gain_a).astype(bf16)
    qkv = lax.dot_general(
        own_in, seq_normed, (((0,), (1,)), ((), ())), preferred_element_type=f32
    ).astype(bf16)

    route_ids = routes[:, 0]
    route_hot = route_ids[:, None] == jnp.arange(experts, dtype=jnp.int32)[None, :]
    hot_counts = route_hot.astype(jnp.int32)
    slot_rank = jnp.sum((jnp.cumsum(hot_counts, axis=0) - 1) * hot_counts, axis=1)
    slot_index = route_ids * capacity + slot_rank
    slots = experts * capacity
    place = (jnp.arange(slots, dtype=jnp.int32)[:, None] == slot_index[None, :]).astype(bf16)

    def dispatch(values):
        placed = jnp.dot(place, values, preferred_element_type=f32).astype(bf16)
        return exchange(placed.reshape(experts, capacity, width), "expert").reshape(slots, width)

    def collect(values):
        returned = exchange(values.reshape(experts, capacity, width), "expert").reshape(slots, width)
        return lax.dot_general(
            place, returned, (((0,), (0,)), ((), ())), preferred_element_type=f32
        )

    weight_in, weight_out = expert_in[0], expert_out[0]
    cot_rows = dispatch(cotangent)
    grad_plain = lax.dot_general(
        cot_rows, weight_out, (((1,), (1,)), ((), ())), preferred_element_type=f32
    )

    chunks = 2 * length // LANES
    offset_ids = jnp.concatenate([jnp.full((1,), -1, jnp.int32), buckets[::-1]])
    offset_table = (offset_ids[:, None] == jnp.arange(bucket_count, dtype=jnp.int32)[None, :]).astype(f32)
    own_bias = lax.dynamic_slice_in_dim(rel_bias, here * heads, heads, 1).astype(f32)
    offsets = jnp.einsum("bh,ob->ho", own_bias, offset_table, precision=highest).reshape(
        heads, chunks, LANES
    )
    mixed_own, logs = attention_forward(offsets, qkv, heads)

    full_out = lax.all_gather(attn_out, "wshard", axis=0, tiled=True)
    full_in = lax.all_gather(
        sorted_in.transpose(1, 0, 2).reshape(part, 3 * width), "wshard", axis=0, tiled=True
    )

    def to_tokens(values):
        pieces = values.reshape(values.shape[0], shards, rows).transpose(1, 0, 2)
        return exchange(pieces, "wshard").reshape(shards * values.shape[0], rows)

    mixed_heads = to_tokens(mixed_own)
    start_rows = tokens.astype(f32)
    branch = lax.dot_general(
        mixed_heads, full_out, (((0,), (0,)), ((), ())), preferred_element_type=f32
    )
    middle = start_rows + branch
    scale_f = rms_scale(middle)
    normed_f = (middle * scale_f * gain_f).astype(bf16)
    arrived = dispatch(normed_f)

    def route_probs(values):
        logits = lax.dot_general(
            values, full_router, (((1,), (1,)), ((), ())), preferred_element_type=f32
        )
        shifted = jnp.exp(logits - jnp.max(logits, axis=-1, keepdims=True))
        return shifted / jnp.sum(shifted, axis=-1, keepdims=True)

    probs = route_probs(arrived)
    own_hot = jnp.arange(experts, dtype=jnp.int32)[None, :] == owner
    gate = jnp.sum(jnp.where(own_hot, probs, 0.0), axis=-1, keepdims=True)
    inner = jnp.dot(arrived, weight_in, preferred_element_type=f32)
    hidden, slope = gelu_parts(inner)
    grad_gate = jnp.sum(hidden * grad_plain, axis=-1, keepdims=True)
    grad_inner = (slope * (gate * grad_plain)).astype(bf16)
    hidden = hidden.astype(bf16)
    grad_logits = (probs * (jnp.where(own_hot, grad_gate, 0.0) - gate * grad_gate)).astype(bf16)
    row_grads = lax.dot_general(
        grad_inner, weight_in, (((1,), (1,)), ((), ())), preferred_element_type=f32
    ) + jnp.dot(grad_logits, full_router, preferred_element_type=f32)
    grad_normed_f = collect(row_grads.astype(bf16))

    results = jnp.dot(hidden, weight_out, preferred_element_type=f32).astype(bf16)
    expert_result = collect(results)
    own_probs = route_probs(normed_f)
    gate_prob = jnp.sum(jnp.where(route_hot, own_probs, 0.0), axis=-1, keepdims=True)
    mixed = (middle + gate_prob * expert_result).astype(bf16)

    grad_result = (gate * cot_rows.astype(f32)).astype(bf16)
    local_out = lax.dot_general(
        hidden, grad_result, (((0,), (0,)), ((), ())), preferred_element_type=f32
    )
    local_in = lax.dot_general(
        arrived, grad_inner, (((0,), (0,)), ((), ())), preferred_element_type=f32
    )
    local_router = lax.dot_general(
        arrived, grad_logits, (((0,), (0,)), ((), ())), preferred_element_type=f32
    )
    grad_expert_in = lax.psum_scatter(
        local_in.astype(bf16), "wshard", scatter_dimension=1, tiled=True
    ).astype(f32)[None]
    grad_expert_out = lax.psum_scatter(
        local_out.astype(bf16), "wshard", scatter_dimension=0, tiled=True
    ).astype(f32)[None]

    grad_out = cotangent.astype(f32)
    grad_middle_norm, grad_gain_f = norm_back(grad_normed_f, middle, scale_f, gain_f)
    grad_middle = grad_out + grad_middle_norm
    grad_branch = grad_middle.astype(bf16)
    grad_mixed = lax.dot_general(
        full_out, grad_branch, (((1,), (1,)), ((), ())), preferred_element_type=f32
    ).astype(bf16)
    grad_own = (
        exchange(grad_mixed.reshape(shards, part, rows), "wshard").transpose(1, 0, 2).reshape(part, length)
    )
    grad_attn_out = jnp.dot(mixed_heads, grad_branch, preferred_element_type=f32)
    grad_query, grad_key, grad_value, grad_offsets = attention_backward(
        offsets, qkv, grad_own, mixed_own, logs, heads
    )
    grad_qkv = jnp.concatenate([grad_query, grad_key, grad_value], axis=0)
    grad_tokens_qkv = to_tokens(grad_qkv)
    grad_normed = lax.dot_general(
        grad_tokens_qkv, full_in, (((0,), (1,)), ((), ())), preferred_element_type=f32
    )
    scale_a = rms_scale(start_rows)
    grad_start, grad_gain_a = norm_back(grad_normed, start_rows, scale_a, gain_a)
    grad_tokens = grad_middle + grad_start

    local_attn_in = lax.dot_general(
        seq_normed, grad_qkv, (((0,), (1,)), ((), ())), preferred_element_type=f32
    )
    summed_in = lax.psum_scatter(local_attn_in, "expert", scatter_dimension=0, tiled=True)
    slim = summed_in.shape[0] // shards
    sum_attn_in = (
        exchange(summed_in.reshape(shards, slim, 3 * part), "wshard")
        .reshape(shards, slim, 3, part)
        .transpose(1, 2, 0, 3)
        .reshape(slim, 3 * width)
    )
    both = ("expert", "wshard")
    sum_attn_out = lax.psum_scatter(grad_attn_out, both, scatter_dimension=0, tiled=True)
    own_offsets = jnp.einsum(
        "ob,ho->bh", offset_table, grad_offsets.reshape(heads, -1), precision=highest
    )
    spread = (jnp.arange(shards) == here).astype(f32)
    local_bias = (own_offsets[:, None, :] * spread[None, :, None]).reshape(bucket_count, head_total)
    grad_rel_bias = lax.psum(local_bias, both)
    sum_gain_a = lax.psum_scatter(grad_gain_a, both, scatter_dimension=0, tiled=True)
    sum_gain_f = lax.psum_scatter(grad_gain_f, both, scatter_dimension=0, tiled=True)
    sum_router = lax.psum_scatter(local_router, both, scatter_dimension=0, tiled=True)
    return (
        mixed,
        grad_tokens,
        sum_gain_a,
        sum_attn_in,
        sum_attn_out,
        grad_rel_bias,
        sum_gain_f,
        sum_router,
        grad_expert_in,
        grad_expert_out,
    )


def solution(mesh):
    placed = (
        P(("expert", "wshard"), None),
        P("wshard"),
        P("wshard", None),
        P("wshard", None),
        P(),
        P(),
        P("wshard"),
        P("wshard", None),
        P(("expert", "wshard"), None),
        P("expert", None, None),
        P("expert", None, None),
        P(("expert", "wshard"), None),
    )
    return jax.shard_map(
        local,
        mesh=mesh,
        in_specs=placed,
        out_specs=(
            P(("expert", "wshard"), None),
            P(("expert", "wshard"), None),
            P(("expert", "wshard")),
            P(("expert", "wshard"), None),
            P(("expert", "wshard"), None),
            P(),
            P(("expert", "wshard")),
            P(("expert", "wshard"), None),
            P("expert", None, "wshard"),
            P("expert", "wshard", None),
        ),
        check_vma=False,
    )
```

time: 2000 us -> 697 us (0.35)
  local copies, waits for them, and re-layouts: 1070 us -> 25 us
  waiting for transfers between devices: 468 us -> 320 us
  matrix products: 250 us -> 111 us
  Pallas kernels: 0 us -> 107 us
  other arithmetic: 106 us -> 29.2 us
  starting transfers between devices: 19.6 us -> 40.9 us
    while x63 -> x0, local copies, waits for them, and re-layouts: 648 us -> none
    reshape x11 -> x13, local copies, waits for them, and re-layouts: 257 us -> 13.4 us  [the longest x2 4.25 us: to_tokens(): pieces = values.reshape(values.shape[0], shards, rows).transpose(1, 0, 2)]
    reduce_scatter x6 -> x4, waiting for transfers between devices: 316 us -> 112 us  [the longest x1 103 us: local(): lax.psum_scatter(grad_attn_out, both, scatter_dimension=0, tiled=True)]
    dot_general x38 -> x22, matrix products: 250 us -> 111 us  [the longest x1 15.2 us: local(): lax.dot_general(cot_rows, weight_out, (((1,), (1,)), ((), ())), preferred...]
    pallas_call x0 -> x2, Pallas kernels: none -> 107 us  [the longest x1 77.4 us: attention_backward(): pl.pallas_call(backward_kernel, grid=(heads,), in_specs=[pl.BlockSpec((1,...]
    all_to_all x4 -> x9, waiting for transfers between devices: 78.8 us -> 176 us  [exchange(): return lax.all_to_all(rows, axis, split_axis=0, concat_axis=0, tiled=True)]
    pad x12 -> x1, local copies, waits for them, and re-layouts: 62.4 us -> 0.01 us  [local(): jnp.pad(small, (0, small_rows * width - small.shape[0]))]
    slice x8 -> x2, local copies, waits for them, and re-layouts: 52 us -> 0.22 us  [the longest x6 49.6 us: expand_offsets(): repeated = jnp.tile(padded, (1, row_count))[:, :row_count * (span - 1)]]
  transfers between devices with their start and end apart: 14 -> 16, of which waited for: 12 -> 10; matrix products, arithmetic and copies ran while one was open for 30% -> 18% of each run, Pallas kernels for 0% -> 16%
where the time goes in v1:
time: 697 us; the launch traced here: 687 us
  waiting for transfers between devices  320 us (46%)
  matrix products  111 us (16%)
  Pallas kernels  107 us (15%)
  starting transfers between devices  40.9 us (6%)
  blocking collectives  39.4 us (6%)
  other arithmetic  29.2 us (4%)
  local copies, waits for them, and re-layouts  25 us (4%)
  between operations  15.1 us (2%)
    all_to_all x9, waiting for transfers between devices, exchange(): return lax.all_to_all(rows, axis, split_axis=0, concat_axis=0, tiled=True)  176 us
    reduce_scatter x1, waiting for transfers between devices, local(): lax.psum_scatter(grad_attn_out, both, scatter_dimension=0, tiled=True)  103 us
    pallas_call x1, Pallas kernels, attention_backward(): pl.pallas_call(backward_kernel, grid=(heads,), in_specs=[pl.BlockSpec((1,...  77.4 us
    all_to_all x9, starting transfers between devices, exchange(): return lax.all_to_all(rows, axis, split_axis=0, concat_axis=0, tiled=True)  40 us
    unnamed x1, blocking collectives  39.4 us
    all_gather x1, waiting for transfers between devices, local(): lax.all_gather(jnp.concatenate([tokens, small], axis=0), 'wshard', axis=0)  31.7 us
    pallas_call x1, Pallas kernels, attention_forward(): pl.pallas_call(forward_kernel, grid=(heads,), in_specs=[pl.BlockSpec((1,...  29.2 us
    dot_general x1, matrix products, local(): lax.dot_general(cot_rows, weight_out, (((1,), (1,)), ((), ())), preferred...  15.2 us
  transfers between devices with their start and end apart: 16, of which 10 were waited for; matrix products, arithmetic and copies ran while one was open for 18% of the time, Pallas kernels for 16%

profile of v1, /device:TPU:0, one launch (start us, length us, event | category | flops | bytes accessed | tf_op | source)
XLA Modules:
  0.0 687.2 jit_solution(14612560406008972742)
XLA Ops:
  15.2 4.2 all-to-all-start
  21.0 31.7 %all-gather.9.cloned.1.call-done = bf16[2112,768]{1,0:T(8,128)(2,1)} async-done(((bf16[528,768]{1,0:T(8,128)(2,1)}), bf16[2112,768]{1,0:T(8,128)(2,1)}) %all-gather.9.cloned.1.call-update) | async-done | bytes 3244048 | tf_op jit(solution)/shard_map/all_gather | solution.py:316
  53.7 2.6 multiply_reduce_fusion.1
  56.6 2.1 multiply_convert_fusion
  58.7 4.2 fusion.21.query_ref.key_ref.value_ref
  62.9 29.2 %shard_map.195 = (bf16[192,2048]{1,0:T(8,128)(2,1)S(1)}, f32[3,1,2048]{2,1,0:T(1,128)S(1)}) custom-call(f32[3,32,128]{2,1,0:T(8,128)S(1)} %bitcast.125, bf16[576,2048]{1,0:T(8,128)(2,1)S(1)} %fusion.21.query_ref.key_ref.value_ref, bf16[576,2048]{1,0:T(8,128)(2,1)S(1)} %fusion.21.query_ref.key_ref.value_ref, ...), custom_call_target="tpu_custom_call" | custom-call | flops 12884901888 | bytes 8388608 | tf_op jit(solution)/shard_map/pallas_call | solution.py:203
  93.1 3.5 all-to-all-start.1
  98.2 10.0 %all-to-all-done.1 = bf16[4,192,512]{2,1,0:T(8,128)(2,1)S(1)} async-done(((bf16[4,192,512]{2,1,0:T(8,128)(2,1)}), bf16[4,192,512]{2,1,0:T(8,128)(2,1)S(1)}, u32[]{:S(2)}, u32[]{:S(2)}) %all-to-all-start.1) | async-done | bytes 786464 | tf_op jit(solution)/shard_map/all_to_all | solution.py:285
  109.1 2.4 multiply_reduce_fusion.4
  111.6 2.3 fusion.26
  113.9 6.7 all-to-all-start.2
  120.6 3.4 fusion.27
  124.0 33.4 %all-to-all-done.2 = bf16[8,128,768]{2,1,0:T(8,128)(2,1)S(1)} async-done(((bf16[8,128,768]{2,1,0:T(8,128)(2,1)}), bf16[8,128,768]{2,1,0:T(8,128)(2,1)S(1)}, u32[]{:S(2)}, u32[]{:S(2)}) %all-to-all-start.2) | async-done | bytes 1572896 | tf_op jit(solution)/shard_map/all_to_all | solution.py:285
  157.4 4.8 all-to-all-start.4
  163.0 10.3 %fusion.19 = f32[1024,3072]{1,0:T(8,128)} fusion(bf16[1024,768]{1,0:T(8,128)(2,1)S(1)} %bitcast.133, bf16[1,768,3072]{2,1,0:T(8,128)(2,1)} %param.21), kind=kOutput, calls=%fused_computation.28 | convolution fusion | flops 4831838208 | bytes 18874368 | tf_op jit(solution)/shard_map/dot_general | solution.py:398
  173.3 25.5 %all-to-all-done.4 = bf16[8,128,768]{2,1,0:T(8,128)(2,1)} async-done(((bf16[8,128,768]{2,1,0:T(8,128)(2,1)}), bf16[8,128,768]{2,1,0:T(8,128)(2,1)}, u32[]{:S(2)}, u32[]{:S(2)}) %all-to-all-start.4) | async-done | bytes 1572896 | tf_op jit(solution)/shard_map/all_to_all | solution.py:285
  198.8 15.2 %multiply_reduce_fusion = (f32[1024]{0:T(1024)S(1)}, bf16[1024,3072]{1,0:T(8,128)(2,1)S(1)}) fusion(f32[1024,3072]{1,0:T(8,128)} %fusion.19, f32[1024]{0:T(1024)S(1)} %select_reduce_fusion, bf16[1024,768]{1,0:T(8,128)(2,1)} %bitcast.21, bf16[1,3072,768]{2,1,0:T(8,128)(2,1)} %param.22), kind=kOutput, calls=%fused_computation.12 | convolution fusion | flops 4901043200 | bytes 25174016 | tf_op jit(solution)/shard_map/dot_general | solution.py:356
  214.0 9.7 %fusion.17 = f32[1024,768]{1,0:T(8,128)S(1)} fusion(bf16[1024,3072]{1,0:T(8,128)(2,1)S(1)} %get-tuple-element.31, bf16[1,768,3072]{2,1,0:T(8,128)(2,1)} %param.21), kind=kOutput, calls=%fused_computation.26 | convolution fusion | flops 4831838208 | bytes 14155776 | tf_op jit(solution)/shard_map/dot_general | solution.py:404
  225.5 4.3 all-to-all-start.5
  230.1 2.3 copy.57
  232.4 5.0 slice_convert_fusion
  237.4 29.0 %all-to-all-done.5 = bf16[8,128,768]{2,1,0:T(8,128)(2,1)} async-done(((bf16[8,128,768]{2,1,0:T(8,128)(2,1)}), bf16[8,128,768]{2,1,0:T(8,128)(2,1)}, u32[]{:S(2)}, u32[]{:S(2)}) %all-to-all-start.5) | async-done | bytes 1572896 | tf_op jit(solution)/shard_map/all_to_all | solution.py:285
  266.5 3.4 multiply_reduce_fusion.2
  271.5 3.1 fusion.39
  274.7 2.3 copy.52
  277.0 4.2 all-to-all-start.6
  281.2 5.1 fusion.11
  286.3 6.6 all-to-all-done.6
  294.1 77.4 %shard_map.196 = (bf16[192,2048]{1,0:T(8,128)(2,1)S(1)}, bf16[192,2048]{1,0:T(8,128)(2,1)S(1)}, bf16[192,2048]{1,0:T(8,128)(2,1)S(1)}, f32[3,32,128]{2,1,0:T(8,128)S(1)}) custom-call(f32[3,32,128]{2,1,0:T(8,128)S(1)} %bitcast.126, bf16[576,2048]{1,0:T(8,128)(2,1)} %copy-done.2, bf16[576,2048]{1,0:T(8,128)(2,1)} %copy-done.2, bf16[576,2048]{1,0:T(8,128)(2,1)} %copy-done.2, ...), custom_call_target="tpu_custom_call" | custom-call | flops 32212254720 | bytes 12582912 | tf_op jit(solution)/shard_map/pallas_call | solution.py:239
  374.2 4.0 fusion.66
  378.5 9.6 %convolution_convert_fusion.1 = bf16[768,3072]{1,0:T(8,128)(2,1)} fusion(bf16[1024,768]{1,0:T(8,128)(2,1)S(1)} %bitcast.134, bf16[1024,3072]{1,0:T(8,128)(2,1)} %copy-done.19), kind=kOutput, calls=%fused_computation.21 | convolution fusion | flops 4834197504 | bytes 12582912 | tf_op jit(solution)/shard_map/dot_general | solution.py:419
  388.2 12.5 %convolution_convert_fusion = bf16[3072,768]{1,0:T(8,128)(2,1)} fusion(bf16[1024,768]{1,0:T(8,128)(2,1)} %bitcast.21, f32[1024]{0:T(1024)S(1)} %select_reduce_fusion, f32[1024,3072]{1,0:T(8,128)} %fusion.19), kind=kOutput, calls=%fused_computation.20 | convolution fusion | flops 4864868352 | bytes 18878464 | tf_op jit(solution)/shard_map/dot_general | solution.py:416
  400.7 12.6 %fusion.28 = bf16[1024,768]{1,0:T(8,128)(2,1)} fusion(bf16[1,3072,768]{2,1,0:T(8,128)(2,1)} %param.22, f32[1024,3072]{1,0:T(8,128)} %fusion.19), kind=kOutput, calls=%fused_computation.48 | convolution fusion | flops 4860936192 | bytes 18874368 | tf_op jit(solution)/shard_map/dot_general | solution.py:409
  413.3 4.3 all-to-all-start.3
  418.0 3.3 copy.74
  421.3 41.4 %all-to-all-done.3 = bf16[8,128,768]{2,1,0:T(8,128)(2,1)} async-done(((bf16[8,128,768]{2,1,0:T(8,128)(2,1)}), bf16[8,128,768]{2,1,0:T(8,128)(2,1)}, u32[]{:S(2)}, u32[]{:S(2)}) %all-to-all-start.3) | async-done | bytes 1572896 | tf_op jit(solution)/shard_map/all_to_all | solution.py:285
  462.7 4.6 all-to-all-start.7
  469.6 4.0 fusion.45
  474.0 4.1 add_convert_fusion.1
  478.5 29.9 %all-to-all-done.7 = bf16[4,576,512]{2,1,0:T(8,128)(2,1)} async-done(((bf16[4,576,512]{2,1,0:T(8,128)(2,1)}), bf16[4,576,512]{2,1,0:T(8,128)(2,1)}, u32[]{:S(2)}, u32[]{:S(2)}) %all-to-all-start.7) | async-done | bytes 2359328 | tf_op jit(solution)/shard_map/all_to_all | solution.py:285
  508.5 5.1 fusion.37
  513.6 3.4 all-to-all-start.8
  517.1 3.0 fusion.34
  520.1 39.4 %all-reduce.4 = (f32[768]{0:T(1024)S(1)}, f32[32,12]{0,1:T(8,128)}, f32[768]{0:T(1024)S(1)}, f32[768,8]{0,1:T(8,128)S(1)}) all-reduce(f32[768]{0:T(1024)S(1)} %get-tuple-element.24, f32[32,12]{0,1:T(8,128)S(1)} %broadcast_multiply_fusion, ...), channel_id=3, replica_groups=mesh['expert'=8,'wshard'=4] {'expert','wshard'}, use_global_device_ids=true, to_apply=%region_16.17.clone | all-reduce | flops 8064 | bytes 64512
  562.6 2.9 bitcast_convert_fusion.1
  565.4 8.6 %reduce-scatter.12.cloned.1.call-done = bf16[768,768]{1,0:T(8,128)(2,1)} async-done(((bf16[3072,768]{1,0:T(8,128)(2,1)}), bf16[768,768]{1,0:T(8,128)(2,1)}) %reduce-scatter.12.cloned.1.call-update) | async-done | bytes 1179664 | tf_op jit(solution)/shard_map/reduce_scatter | solution.py:428
  574.1 2.8 bitcast_convert_fusion
  576.9 102.9 %reduce-scatter.8.cloned.1.call-done = f32[24,768]{1,0:T(8,128)} async-done(((f32[768,768]{1,0:T(8,128)}), f32[24,768]{1,0:T(8,128)}) %reduce-scatter.8.cloned.1.call-update) | async-done | bytes 73744 | tf_op jit(solution)/shard_map/reduce_scatter | solution.py:467
  (125 shorter events, 29.6 us)
Async XLA Ops:
  7.2 13.2 %copy-start = (bf16[32,12]{0,1:T(8,128)(2,1)S(1)}, bf16[32,12]{0,1:T(8,128)(2,1)}, u32[]{:S(2)}) copy-start(bf16[32,12]{0,1:T(8,128)(2,1)} %param.16) | copy-start | bytes 2308
  7.2 4.5 copy-start.12
  7.2 45.5 %all-gather.9.cloned.1.call-start = ((), (), s32[]{:S(2)}) async-start(), calls=%async_computation.19 | async-start | bytes 4055040 | tf_op jit(solution)/shard_map/all_gather | solution.py:316
  13.8 6.6 copy-start.4
  13.8 6.4 copy-start.15
  15.2 43.5 %all-to-all-start = ((bf16[4,192,576]{2,1,0:T(8,128)(2,1)}), bf16[4,192,576]{2,1,0:T(8,128)(2,1)}, u32[]{:S(2)}, u32[]{:S(2)}) async-start(bf16[4,192,576]{2,1,0:T(8,128)(2,1)} %copy.49), calls=%async_computation | async-start | bytes 1966080 | tf_op jit(solution)/shard_map/all_to_all | solution.py:285
  19.4 78.8 %all-gather.5.cloned.1.call-start = ((), (), s32[]{:S(2)}) async-start(), calls=%async_computation.13 | async-start | bytes 1474560 | tf_op jit(solution)/shard_map/all_gather | solution.py:369
  20.4 0.6 copy-start.16
  52.7 3.9 copy-start.3
  62.9 29.3 %copy-start.2 = (bf16[576,2048]{1,0:T(8,128)(2,1)}, bf16[576,2048]{1,0:T(8,128)(2,1)S(1)}, u32[]{:S(2)}) copy-start(bf16[576,2048]{1,0:T(8,128)(2,1)S(1)} %fusion.21.query_ref.key_ref.value_ref) | copy-start | bytes 7077892
  92.1 4.5 copy-start.14
  92.1 17.0 %copy-start.5 = (bf16[512,768]{1,0:T(8,128)(2,1)S(1)}, bf16[512,768]{1,0:T(8,128)(2,1)}, u32[]{:S(2)}) copy-start(bf16[512,768]{1,0:T(8,128)(2,1)} %param.12) | copy-start | bytes 2359300
  93.1 15.1 %all-to-all-start.1 = ((bf16[4,192,512]{2,1,0:T(8,128)(2,1)}), bf16[4,192,512]{2,1,0:T(8,128)(2,1)S(1)}, u32[]{:S(2)}, u32[]{:S(2)}) async-start(bf16[4,192,512]{2,1,0:T(8,128)(2,1)} %bitcast.121), calls=%async_computation.1 | async-start | bytes 1572864 | tf_op jit(solution)/shard_map/all_to_all | solution.py:285
  108.2 0.9 copy-start.10
  111.5 2.4 copy-start.6
  113.9 43.5 %all-to-all-start.2 = ((bf16[8,128,768]{2,1,0:T(8,128)(2,1)}), bf16[8,128,768]{2,1,0:T(8,128)(2,1)S(1)}, u32[]{:S(2)}, u32[]{:S(2)}) async-start(bf16[8,128,768]{2,1,0:T(8,128)(2,1)} %bitcast.147), calls=%async_computation.2 | async-start | bytes 3145728 | tf_op jit(solution)/shard_map/all_to_all | solution.py:285
  157.4 41.4 %all-to-all-start.4 = ((bf16[8,128,768]{2,1,0:T(8,128)(2,1)}), bf16[8,128,768]{2,1,0:T(8,128)(2,1)}, u32[]{:S(2)}, u32[]{:S(2)}) async-start(bf16[8,128,768]{2,1,0:T(8,128)(2,1)} %bitcast.145), calls=%async_computation.4 | async-start | bytes 3145728 | tf_op jit(solution)/shard_map/all_to_all | solution.py:285
  214.0 9.7 %copy-start.19 = (bf16[1024,3072]{1,0:T(8,128)(2,1)}, bf16[1024,3072]{1,0:T(8,128)(2,1)S(1)}, u32[]{:S(2)}) copy-start(bf16[1024,3072]{1,0:T(8,128)(2,1)S(1)} %get-tuple-element.31) | copy-start | bytes 18874372
  225.5 40.9 %all-to-all-start.5 = ((bf16[8,128,768]{2,1,0:T(8,128)(2,1)}), bf16[8,128,768]{2,1,0:T(8,128)(2,1)}, u32[]{:S(2)}, u32[]{:S(2)}) async-start(bf16[8,128,768]{2,1,0:T(8,128)(2,1)} %bitcast.139), calls=%async_computation.5 | async-start | bytes 3145728 | tf_op jit(solution)/shard_map/all_to_all | solution.py:285
  229.8 248.7 %all-gather.7.cloned.1.call-start = ((), (), s32[]{:S(2)}) async-start(), calls=%async_computation.14 | async-start | bytes 4423680 | tf_op jit(solution)/shard_map/all_gather | solution.py:370
  266.5 3.4 copy-start.7
  266.5 3.4 copy-start.13
  269.9 1.6 copy-start.18
  277.0 15.9 %all-to-all-start.6 = ((bf16[4,192,512]{2,1,0:T(8,128)(2,1)}), bf16[4,192,512]{2,1,0:T(8,128)(2,1)}, u32[]{:S(2)}, u32[]{:S(2)}) async-start(bf16[4,192,512]{2,1,0:T(8,128)(2,1)} %bitcast.143), calls=%async_computation.6 | async-start | bytes 1572864 | tf_op jit(solution)/shard_map/all_to_all | solution.py:285
  281.1 232.5 %reduce-scatter.6.cloned.1.call-start = ((), (), s32[]{:S(2)}) async-start(), calls=%async_computation.15 | async-start | bytes 2211840 | tf_op jit(solution)/shard_map/reduce_scatter | solution.py:458
  371.4 2.7 copy-start.9
  371.7 1.4 copy-start.8
  378.2 184.3 %reduce-scatter.10.cloned.1.call-start = ((), (), s32[]{:S(2)}) async-start(), calls=%async_computation.17 | async-start | bytes 5898240 | tf_op jit(solution)/shard_map/reduce_scatter | solution.py:425
  388.1 185.9 %reduce-scatter.12.cloned.1.call-start = ((), (), s32[]{:S(2)}) async-start(), calls=%async_computation.18 | async-start | bytes 5898240 | tf_op jit(solution)/shard_map/reduce_scatter | solution.py:428
  413.3 49.4 %all-to-all-start.3 = ((bf16[8,128,768]{2,1,0:T(8,128)(2,1)}), bf16[8,128,768]{2,1,0:T(8,128)(2,1)}, u32[]{:S(2)}, u32[]{:S(2)}) async-start(bf16[8,128,768]{2,1,0:T(8,128)(2,1)} %bitcast.146), calls=%async_computation.3 | async-start | bytes 3145728 | tf_op jit(solution)/shard_map/all_to_all | solution.py:285
  462.7 6.9 copy-start.11
  462.7 45.7 %all-to-all-start.7 = ((bf16[4,576,512]{2,1,0:T(8,128)(2,1)}), bf16[4,576,512]{2,1,0:T(8,128)(2,1)}, u32[]{:S(2)}, u32[]{:S(2)}) async-start(bf16[4,576,512]{2,1,0:T(8,128)(2,1)} %bitcast.138), calls=%async_computation.7 | async-start | bytes 4718592 | tf_op jit(solution)/shard_map/all_to_all | solution.py:285
  467.3 212.5 %reduce-scatter.8.cloned.1.call-start = ((), (), s32[]{:S(2)}) async-start(), calls=%async_computation.16 | async-start | bytes 2433024 | tf_op jit(solution)/shard_map/reduce_scatter | solution.py:467
  474.0 4.1 copy-start.17
  513.6 47.7 %all-to-all-start.8 = ((f32[4,24,576]{2,1,0:T(8,128)}), f32[4,24,576]{2,1,0:T(8,128)S(1)}, u32[]{:S(2)}, u32[]{:S(2)}) async-start(f32[4,24,576]{2,1,0:T(8,128)} %bitcast.149), calls=%async_computation.9 | async-start | bytes 491520 | tf_op jit(solution)/shard_map/all_to_all | solution.py:285
  562.6 117.3 %copy-start.1 = (bf16[32,12]{0,1:T(8,128)(2,1)S(1)}, bf16[32,12]{0,1:T(8,128)(2,1)}, u32[]{:S(2)}) copy-start(bf16[32,12]{0,1:T(8,128)(2,1)} %param.16) | copy-start | bytes 2308
Sparse Core Ops, SparseCore 0:
  11.8 40.8 all-gather.8
  54.2 18.6 all-gather.4
  232.5 31.1 all-gather.6
  378.4 85.2 reduce-scatter.5
  466.2 56.9 reduce-scatter.9
  525.6 48.4 reduce-scatter.11
  580.8 99.0 reduce-scatter.7
